TPU v7x, 32 devices: a whole 2x2x4 slice. The times are simulated.
32 devices in a mesh: gx: 16 (over z, y, core), gy: 2 (over x).
Axes of the slice: x: 2, y: 2, z: 4, core: 2. Of those that a mesh axis runs over, the one named last changes fastest.
Arguments:
- latents: int32 [768, 64, 32], P('gy', 'gx'), may hold values from 0 to 31
- actions: int32 [768, 64], P('gy', 'gx'), may hold values from 0 to 17
- segment_ids: int32 [768, 64], replicated, may hold values from 0 to 3, never falling along the last dimension, each value on 1 to 32 neighbouring positions
- cotangent: bfloat16 [768, 64, 512], P('gy', 'gx'), may hold values from -6 to 6
- stem_weight: bfloat16 [1024, 512], replicated, may hold values from -1 to 1
- action_table: bfloat16 [18, 512], replicated, may hold values from -1 to 1
- first_gain: float32 [512], replicated, may hold values from 0.5 to 1.5
- first_bias: float32 [512], replicated, may hold values from -1 to 1
- query_weight: bfloat16 [512, 512], P(None, 'gy'), may hold values from -0.25 to 0.25
- key_weight: bfloat16 [512, 512], P(None, 'gy'), may hold values from -0.25 to 0.25
- value_weight: bfloat16 [512, 512], P(None, 'gy'), may hold values from -0.25 to 0.25
- out_weight: bfloat16 [512, 512], P('gy'), may hold values from -1 to 1
- second_gain: float32 [512], replicated, may hold values from 0.5 to 1.5
- second_bias: float32 [512], replicated, may hold values from -1 to 1
- up_weight: bfloat16 [512, 2048], P(None, 'gy'), may hold values from -0.25 to 0.25
- up_bias: float32 [2048], P('gy'), may hold values from -1 to 1
- down_weight: bfloat16 [2048, 512], P('gy'), may hold values from -0.125 to 0.125
- down_bias: float32 [512], replicated, may hold values from -1 to 1
Outputs:
- output: bfloat16 [768, 64, 512], P('gy', 'gx')
- token_grad: bfloat16 [768, 64, 512], P('gy', 'gx')
- stem_grad: float32 [1024, 512], replicated
- action_grad: float32 [18, 512], replicated
- first_gain_grad: float32 [512], replicated
- first_bias_grad: float32 [512], replicated
- query_grad: float32 [512, 512], P(None, 'gy')
- key_grad: float32 [512, 512], P(None, 'gy')
- value_grad: float32 [512, 512], P(None, 'gy')
- out_grad: float32 [512, 512], P('gy')
- second_gain_grad: float32 [512], replicated
- second_bias_grad: float32 [512], replicated
- up_grad: float32 [512, 2048], P(None, 'gy')
- up_bias_grad: float32 [2048], P('gy')
- down_grad: float32 [2048, 512], P('gy')
- down_bias_grad: float32 [512], replicated
Inputs may be any that keep to these rules, and one draw needn't show every extreme that they name: `segment_ids`: along each sequence of 64 frames the segment id never falls; each segment holds 1 to 32 frames.
All inputs are finite; a program needn't handle non-finite values.
Results may differ from a plain program's by a relative error of at most 0.012.
Values may be sent and summed in bfloat16 or wider, within the bound.
A program may use at most 192 MiB of HBM per device.

v0:
```python
import jax
import jax.numpy as jnp
from jax import lax
from jax.sharding import PartitionSpec as P

HD = 64
EPSILON = 1e-05
FLOAT = jnp.float32
BFLOAT = jnp.bfloat16


def norm_rows(values, gain, bias):
    average = jnp.mean(values, axis=-1, keepdims=True)
    centred = values - average
    spread = jnp.mean(centred * centred, axis=-1, keepdims=True)
    return centred * lax.rsqrt(spread + EPSILON) * gain + bias


def inner(left, right):
    return lax.dot_general(left, right, (((0,), (0,)), ((), ())), preferred_element_type=FLOAT)


def outer(left, right):
    return lax.dot_general(left, right, (((1,), (1,)), ((), ())), preferred_element_type=FLOAT)


def product(left, right):
    return jnp.dot(left, right, preferred_element_type=FLOAT)


def split_heads(block):
    return block.reshape(block.shape[0], block.shape[1], -1, HD)


def block_probs(query_block, key_block, label_block):
    length = query_block.shape[1]
    scores = 0.125 * jnp.einsum(
        "sqhd,skhd->shqk",
        split_heads(query_block),
        split_heads(key_block),
        preferred_element_type=FLOAT,
    )
    place = jnp.arange(length)
    allowed = (label_block[:, :, None] == label_block[:, None, :]) & (
        place[:, None] >= place[None, :]
    )[None]
    return jax.nn.softmax(jnp.where(allowed[:, None], scores, -1e30), axis=-1)


def block_forward(pieces):
    query_block, key_block, value_block, label_block = pieces
    probs_low = block_probs(query_block, key_block, label_block).astype(BFLOAT)
    mixed = jnp.einsum(
        "shqk,skhd->sqhd", probs_low, split_heads(value_block), preferred_element_type=FLOAT
    )
    return mixed.reshape(query_block.shape[0], query_block.shape[1], -1).astype(BFLOAT)


def block_backward(pieces):
    query_block, key_block, value_block, label_block, grad_block = pieces
    probs = block_probs(query_block, key_block, label_block)
    grad_heads = split_heads(grad_block)
    grad_probs = jnp.einsum(
        "sqhd,skhd->shqk", grad_heads, split_heads(value_block), preferred_element_type=FLOAT
    )
    grad_probs = lax.optimization_barrier(grad_probs.astype(BFLOAT)).astype(FLOAT)
    centre = jnp.sum(probs * grad_probs, axis=-1, keepdims=True)
    grad_scores = (probs * (grad_probs - centre)).astype(BFLOAT)
    grad_query = 0.125 * jnp.einsum(
        "shqk,skhd->sqhd", grad_scores, split_heads(key_block), preferred_element_type=FLOAT
    )
    grad_key = 0.125 * jnp.einsum(
        "shqk,sqhd->skhd", grad_scores, split_heads(query_block), preferred_element_type=FLOAT
    )
    grad_value = jnp.einsum(
        "shqk,sqhd->skhd", probs.astype(BFLOAT), grad_heads, preferred_element_type=FLOAT
    )
    shape = (query_block.shape[0], query_block.shape[1], -1)
    return tuple(
        (item.reshape(shape).astype(BFLOAT) for item in (grad_query, grad_key, grad_value))
    )


def layer_pass(seq_tokens, seq_cot, seg_rows, weights):
    (
        first_gain,
        first_bias,
        query_weight,
        key_weight,
        value_weight,
        out_weight,
        second_gain,
        second_bias,
        up_weight,
        up_bias,
        down_weight,
        down_bias,
    ) = weights
    seqs, length, width = seq_tokens.shape
    rows = seqs * length
    block = min(512, rows)
    blocks = rows // block
    within = block // length
    scale = 0.5
    inputs = seq_tokens.reshape(rows, width).astype(FLOAT)
    normed_one = norm_rows(inputs, first_gain, first_bias).astype(BFLOAT)
    query = product(normed_one, query_weight).astype(BFLOAT)
    key_rows = product(normed_one, key_weight).astype(BFLOAT)
    value_rows = product(normed_one, value_weight).astype(BFLOAT)
    labels = seg_rows.reshape(blocks, within, length)

    def split_rows(array):
        return array.reshape(blocks, within, length, -1)

    mixed = lax.map(
        block_forward, (split_rows(query), split_rows(key_rows), split_rows(value_rows), labels)
    )
    mixed = mixed.reshape(rows, -1)
    branch = product(mixed, out_weight)
    branch = lax.psum(branch, "gy")
    resid = inputs + branch
    normed_two = norm_rows(resid, second_gain, second_bias).astype(BFLOAT)
    pre_act = product(normed_two, up_weight) + up_bias
    hidden = jax.nn.gelu(pre_act).astype(BFLOAT)
    out_part = scale * (resid + down_bias) + product(hidden, down_weight)
    cot_rows = seq_cot.reshape(rows, width)
    cot_float = cot_rows.astype(FLOAT)
    down_bias_part = jnp.sum(cot_float, axis=0)
    down_part = inner(hidden, cot_rows)
    d_hidden = outer(cot_rows, down_weight)
    act_input = product(normed_two, up_weight) + up_bias
    _, gelu_pull = jax.vjp(jax.nn.gelu, act_input)
    d_pre = gelu_pull(d_hidden)[0].astype(BFLOAT)
    up_bias_part = jnp.sum(d_pre.astype(FLOAT), axis=0)
    up_part = inner(normed_two, d_pre)
    d_normed_two = outer(d_pre, up_weight)
    d_normed_two = lax.psum(d_normed_two, "gy")
    _, second_pull = jax.vjp(norm_rows, resid, second_gain, second_bias)
    d_resid_norm, second_gain_part, second_bias_part = second_pull(d_normed_two)
    d_resid = cot_float + d_resid_norm
    d_branch = d_resid.astype(BFLOAT)
    out_part_grad = inner(mixed, d_branch)
    d_mixed = outer(d_branch, out_weight).astype(BFLOAT)
    d_query, d_key, d_value = lax.map(
        block_backward,
        (
            split_rows(query),
            split_rows(key_rows),
            split_rows(value_rows),
            labels,
            split_rows(d_mixed),
        ),
    )
    d_query = d_query.reshape(rows, -1)
    d_key = d_key.reshape(rows, -1)
    d_value = d_value.reshape(rows, -1)
    query_part = inner(normed_one, d_query)
    key_part = inner(normed_one, d_key)
    value_part = inner(normed_one, d_value)
    d_normed_one = (
        outer(d_query, query_weight) + outer(d_key, key_weight) + outer(d_value, value_weight)
    )
    _, first_pull = jax.vjp(norm_rows, inputs, first_gain, first_bias)
    d_input_norm, first_gain_part, first_bias_part = first_pull(d_normed_one)
    d_tokens_part = scale * d_resid + d_input_norm
    parts = (
        first_gain_part,
        first_bias_part,
        query_part,
        key_part,
        value_part,
        out_part_grad,
        second_gain_part,
        second_bias_part,
        up_part,
        up_bias_part,
        down_part,
        down_bias_part,
    )
    return (
        out_part.reshape(seqs, length, width),
        d_tokens_part.reshape(seqs, length, width),
        parts,
    )


def per_device(
    latents,
    actions,
    segment_ids,
    cotangent,
    stem_weight,
    action_table,
    first_gain,
    first_bias,
    query_weight,
    key_weight,
    value_weight,
    out_weight,
    second_gain,
    second_bias,
    up_weight,
    up_bias,
    down_weight,
    down_bias,
):
    half_seqs, local_len, groups = latents.shape
    frames = half_seqs * local_len
    classes = stem_weight.shape[0] // groups
    latent_hot = (latents[..., None] == jnp.arange(classes, dtype=jnp.int32)).reshape(
        frames, groups * classes
    )
    latent_hot = latent_hot.astype(BFLOAT)
    action_hot = (
        actions.reshape(frames, 1) == jnp.arange(action_table.shape[0], dtype=jnp.int32)[None, :]
    )
    action_hot = action_hot.astype(BFLOAT)
    stem = product(latent_hot, stem_weight) + product(action_hot, action_table)
    tokens = stem.astype(BFLOAT).reshape(half_seqs, local_len, -1)
    token_all, cot_all = (
        lax.all_gather(tokens, "gy", axis=0, tiled=True),
        lax.all_gather(cotangent, "gy", axis=0, tiled=True),
    )
    seq_tokens, seq_cot = (
        lax.all_to_all(token_all, "gx", split_axis=0, concat_axis=1, tiled=True),
        lax.all_to_all(cot_all, "gx", split_axis=0, concat_axis=1, tiled=True),
    )
    seqs = seq_tokens.shape[0]
    first_seq = lax.axis_index("gx") * seqs
    weights = (
        first_gain,
        first_bias,
        query_weight,
        key_weight,
        value_weight,
        out_weight,
        second_gain,
        second_bias,
        up_weight,
        up_bias,
        down_weight,
        down_bias,
    )
    seg_rows = lax.dynamic_slice_in_dim(segment_ids, first_seq, seqs, 0)
    out_seq, grad_seq, parts = layer_pass(seq_tokens, seq_cot, seg_rows, weights)
    out_moved, grad_moved = (
        lax.all_to_all(out_seq, "gx", split_axis=1, concat_axis=0, tiled=True),
        lax.all_to_all(grad_seq, "gx", split_axis=1, concat_axis=0, tiled=True),
    )
    out_frames, grad_frames = (
        lax.psum_scatter(out_moved, "gy", scatter_dimension=0, tiled=True),
        lax.psum_scatter(grad_moved, "gy", scatter_dimension=0, tiled=True),
    )
    output = out_frames.astype(BFLOAT)
    token_grad = grad_frames.astype(BFLOAT)
    width = stem_weight.shape[1]
    grad_flat = token_grad.reshape(frames, width)
    stem_part = inner(latent_hot, grad_flat)
    action_part = inner(action_hot, grad_flat)
    (
        first_gain_part,
        first_bias_part,
        query_part,
        key_part,
        value_part,
        out_part_grad,
        second_gain_part,
        second_bias_part,
        up_part,
        up_bias_part,
        down_part,
        down_bias_part,
    ) = parts
    stem_grad, action_grad, first_gain_grad, first_bias_grad = lax.psum(
        (stem_part, action_part, first_gain_part, first_bias_part), ("gx", "gy")
    )
    (
        query_grad,
        key_grad,
        value_grad,
        out_grad,
        second_gain_grad,
        second_bias_grad,
        up_grad,
        up_bias_grad,
        down_grad,
        down_bias_grad,
    ) = lax.psum(
        (
            query_part,
            key_part,
            value_part,
            out_part_grad,
            second_gain_part,
            second_bias_part,
            up_part,
            up_bias_part,
            down_part,
            down_bias_part,
        ),
        "gx",
    )
    return (
        output,
        token_grad,
        stem_grad,
        action_grad,
        first_gain_grad,
        first_bias_grad,
        query_grad,
        key_grad,
        value_grad,
        out_grad,
        second_gain_grad,
        second_bias_grad,
        up_grad,
        up_bias_grad,
        down_grad,
        down_bias_grad,
    )


def solution(mesh):
    return jax.shard_map(
        per_device,
        mesh=mesh,
        in_specs=(
            P("gy", "gx", None),
            P("gy", "gx"),
            P(),
            P("gy", "gx", None),
            P(),
            P(),
            P(),
            P(),
            P(None, "gy"),
            P(None, "gy"),
            P(None, "gy"),
            P("gy", None),
            P(),
            P(),
            P(None, "gy"),
            P("gy"),
            P("gy", None),
            P(),
        ),
        out_specs=(
            P("gy", "gx", None),
            P("gy", "gx", None),
            P(),
            P(),
            P(),
            P(),
            P(None, "gy"),
            P(None, "gy"),
            P(None, "gy"),
            P("gy", None),
            P(),
            P(),
            P(None, "gy"),
            P("gy"),
            P("gy", None),
            P(),
        ),
        check_vma=False,
    )
```

profile of v0, /device:TPU:0, one launch (start us, length us, event | category | flops | bytes accessed | tf_op | source)
XLA Modules:
  0.0 1381.9 jit_solution(16798744642058293899)
XLA Ops:
  8.6 9.8 eq.86
  18.4 19.9 %eq.87 = s32[1536,1024]{1,0:T(8,128)} reshape(s32[384,4,32,32]{3,2,1,0:T(8,128)} %eq.86) | data formatting | bytes 12582912 | tf_op jit(solution)/shard_map/eq | solution.py:210
  46.1 47.8 %all-gather.3.cloned.1.call-done = bf16[768,4,512]{2,1,0:T(4,128)(2,1)} async-done(((bf16[384,4,512]{2,1,0:T(4,128)(2,1)}), bf16[768,4,512]{2,1,0:T(4,128)(2,1)}) %all-gather.3.cloned.1.call-update) | async-done | bytes 3145744 | tf_op jit(solution)/shard_map/all_gather | solution.py:221
  101.8 57.1 %all-to-all-done = bf16[768,4,512]{2,1,0:T(4,128)(2,1)} async-done(((bf16[768,4,512]{2,1,0:T(4,128)(2,1)}), bf16[768,4,512]{2,1,0:T(4,128)(2,1)}, u32[]{:S(2)}, u32[]{:S(2)}) %all-to-all-start) | async-done | bytes 3145760 | tf_op jit(solution)/shard_map/all_to_all | solution.py:225
  193.5 43.5 %while.24 = (s32[]{:T(128)}, bf16[6,8,64,256]{3,2,1,0:T(8,128)(2,1)}, bf16[6,8,64,256]{3,2,1,0:T(8,128)(2,1)}, s32[6,8,64]{2,1,0:T(8,128)S(1)}, bf16[6,8,64,256]...) while((s32[]{:T(128)}, bf16[6,8,64,256]{3,2,1,0:T(8,128)(2,1)}, ...), condition=%wide.region_5.6_spmd, body=%wide.region_2.5_spmd.sunk | while | flops 34674816 | bytes 9009781 | solution.py:115
  242.1 85.4 %all_to_all.60 = bf16[768,4,512]{2,1,0:T(4,128)(2,1)S(1)} all-to-all(bf16[768,4,512]{2,1,0:T(4,128)(2,1)} %all-gather.5.cloned.1.call-done), channel_id=1, replica_groups=mesh['gx'=16,'gy'=2] {'gx'}, dimensions={0} | all-to-all | bytes 6291456 | tf_op jit(solution)/shard_map/all_to_all | solution.py:226
  338.2 67.0 %all-reduce.12.cloned.1.call-done = f32[3072,512]{1,0:T(8,128)} async-done(((f32[3072,512]{1,0:T(8,128)}), f32[3072,512]{1,0:T(8,128)}) %all-reduce.12.cloned.1.call-update) | async-done | bytes 6291472 | tf_op jit(solution)/shard_map/psum | solution.py:120
  412.7 9.9 multiply_convert_fusion
  422.7 13.3 convert_reduce_fusion
  445.0 9.6 multiply_add_fusion
  467.1 130.6 %all-reduce.14.cloned.1.call-done = f32[3072,512]{1,0:T(8,128)} async-done(((f32[3072,512]{1,0:T(8,128)}), f32[3072,512]{1,0:T(8,128)}) %all-reduce.14.cloned.1.call-update) | async-done | bytes 6291472 | tf_op jit(solution)/shard_map/psum | solution.py:137
  618.5 89.6 %while.25 = (s32[]{:T(128)}, bf16[6,8,64,256]{3,2,1,0:T(8,128)(2,1)}, bf16[6,8,64,256]{3,2,1,0:T(8,128)(2,1)}, bf16[6,8,64,256]{3,2,1,0:T(8,128)(2,1)}, bf16[6,8...) while((s32[]{:T(128)}, ...), condition=%wide.region_17.18_spmd, body=%wide.region_13.17_spmd.sunk | while | flops 86839424 | bytes 17955988 | solution.py:144
  716.4 8.2 multiply_reduce_fusion.1
  744.0 9.9 iota_compare_fusion.2
  753.9 15.2 %eq.98 = pred[1536,1024]{1,0:T(32,128)(4,1)} reshape(pred[384,4,32,32]{3,2,1,0:T(32,128)(4,1)} %iota_compare_fusion.2) | data formatting | bytes 3145728 | tf_op jit(solution)/shard_map/eq | solution.py:210
  781.7 8.6 fusion.55
  790.3 7.8 fusion.39
  805.8 9.7 copy.109
  815.5 58.3 %all-to-all-done.3 = f32[48,64,512]{2,0,1:T(8,128)} async-done(((f32[48,64,512]{2,0,1:T(8,128)}), f32[48,64,512]{2,0,1:T(8,128)}, u32[]{:S(2)}, u32[]{:S(2)}) %all-to-all-start.3) | async-done | bytes 6291488 | tf_op jit(solution)/shard_map/all_to_all | solution.py:248
  873.8 9.6 copy.114
  883.4 290.4 %all-reduce.19 = (bf16[768,4,512]{2,1,0:T(4,128)(2,1)}, bf16[768,4,512]{2,1,0:T(4,128)(2,1)}) all-reduce(f32[768,4,512]{2,1,0:T(4,128)} %bitcast.176, f32[768,4,512]{2,1,0:T(4,128)} %bitcast.177), channel_id=2, replica_groups=mesh['gx'=16,'gy'=2] {'gy'}, use_global_device_ids=true, to_apply=%region_9.10.clone | all-reduce | flops 3145728 | bytes 18874368
  1187.1 102.3 %all-reduce.3 = (f32[512]{0:T(512)}, f32[512]{0:T(512)}, f32[1024]{0:T(1024)}, f32[512]{0:T(512)}) all-reduce(f32[512]{0:T(512)S(1)} %get-tuple-element.146, f32[512]{0:T(512)S(1)} %get-tuple-element.150, f32[1024]{0:T(1024)S(1)} %copy-done.49, f32[512]{0:T(512)S(1)} %convert_reduce_fusion.1), channel_id=1, replica_groups=mesh['gx'=16,'gy'=2] {'gx'}, use_global_device_ids=true, to_apply=%region_32.33 | all-reduce | flops 2560 | bytes 20480 | tf_op jit(solution)/shard_map/psum | solution.py:288
  1289.9 37.9 %all-reduce.2 = (f32[18,512]{1,0:T(8,128)}, f32[512]{0:T(512)}, f32[512]{0:T(512)}) all-reduce(f32[18,512]{1,0:T(8,128)S(1)} %fusion.33, f32[512]{0:T(512)S(1)} %get-tuple-element.148, f32[512]{0:T(512)S(1)} %get-tuple-element.151), channel_id=1, replica_groups=mesh['gx'=16,'gy'=2] {'gx','gy'}, use_global_device_ids=true, to_apply=%region_22.23 | all-reduce | flops 10240 | bytes 81920 | tf_op jit(solution)/shard_map/psum | solution.py:274
  1331.0 32.4 %all-reduce.16.cloned.1.call-done = f32[1024,512]{1,0:T(8,128)} async-done(((f32[1024,512]{1,0:T(8,128)}), f32[1024,512]{1,0:T(8,128)}) %all-reduce.16.cloned.1.call-update) | async-done | bytes 2097168 | tf_op jit(solution)/shard_map/psum | solution.py:274
  (472 shorter events, 323.8 us)
Async XLA Ops:
  7.2 405.5 %copy-start = (bf16[512,1024]{1,0:T(8,128)(2,1)S(1)}, bf16[512,1024]{1,0:T(8,128)(2,1)}, u32[]{:S(2)}) copy-start(bf16[512,1024]{1,0:T(8,128)(2,1)} %param.36) | copy-start | bytes 3145732
  7.2 86.7 %all-gather.3.cloned.1.call-start = ((), (), s32[]{:S(2)}) async-start(), calls=%async_computation.4 | async-start | bytes 4718592 | tf_op jit(solution)/shard_map/all_gather | solution.py:221
  18.4 20.0 %copy-start.48 = (s32[384,4]{0,1:T(4,128)S(1)}, s32[384,4]{0,1:T(4,128)}, u32[]{:S(2)}) copy-start(s32[384,4]{0,1:T(4,128)} %param.23) | copy-start | bytes 18436
  93.9 65.1 %all-to-all-start = ((bf16[768,4,512]{2,1,0:T(4,128)(2,1)}), bf16[768,4,512]{2,1,0:T(4,128)(2,1)}, u32[]{:S(2)}, u32[]{:S(2)}) async-start(bf16[768,4,512]{2,1,0:T(4,128)(2,1)} %all-gather.3.cloned.1.call-done), calls=%async_computation | async-start | bytes 6291456 | tf_op jit(solution)/shard_map/all_to_all | solution.py:225
  99.5 142.6 %all-gather.5.cloned.1.call-start = ((), (), s32[]{:S(2)}) async-start(), calls=%async_computation.6 | async-start | bytes 4718592 | tf_op jit(solution)/shard_map/all_gather | solution.py:222
  100.3 304.9 %all-reduce.12.cloned.1.call-start = ((), (), s32[]{:S(2)}) async-start(), calls=%async_computation.5 | async-start | bytes 12582912 | tf_op jit(solution)/shard_map/psum | solution.py:120
  166.9 15.1 %copy-start.34 = (f32[3072]{0:T(1024)}, f32[3072]{0:T(1024)S(1)}, u32[]{:S(2)}) copy-start(f32[3072]{0:T(1024)S(1)} %div.59) | copy-start | bytes 36868
  193.5 43.5 %copy-start.30 = (bf16[256,512]{1,0:T(8,128)(2,1)S(1)}, bf16[256,512]{1,0:T(8,128)(2,1)}, u32[]{:S(2)}) copy-start(bf16[256,512]{1,0:T(8,128)(2,1)} %param.33) | copy-start | bytes 786436
  242.0 355.7 %all-reduce.14.cloned.1.call-start = ((), (), s32[]{:S(2)}) async-start(), calls=%async_computation.7 | async-start | bytes 12582912 | tf_op jit(solution)/shard_map/psum | solution.py:137
  410.5 12.2 copy-start.3
  461.0 277.1 %all-to-all-start.1 = ((f32[48,64,512]{2,0,1:T(8,128)}), f32[48,64,512]{2,0,1:T(8,128)}, u32[]{:S(2)}, u32[]{:S(2)}) async-start(f32[48,64,512]{2,0,1:T(8,128)} %copy.108), calls=%async_computation.1 | async-start | bytes 12582912 | tf_op jit(solution)/shard_map/all_to_all | solution.py:247
  710.8 19.4 %slice-start.4 = ((s8[6291456]{0:T(1024)(128)(4,1)}), s8[4194304]{0:T(1024)(128)(4,1)S(1)}, s32[]{:S(2)}) async-start(s8[6291456]{0:T(1024)(128)(4,1)} %bitcast.170), calls=%async_computation.14 | async-start | bytes 8388608
  716.4 13.8 slice-start.5
  738.1 135.6 %all-to-all-start.3 = ((f32[48,64,512]{2,0,1:T(8,128)}), f32[48,64,512]{2,0,1:T(8,128)}, u32[]{:S(2)}, u32[]{:S(2)}) async-start(f32[48,64,512]{2,0,1:T(8,128)} %copy.113), calls=%async_computation.3 | async-start | bytes 12582912 | tf_op jit(solution)/shard_map/all_to_all | solution.py:248
  743.9 587.0 %all-reduce.18.cloned.1.call-start = ((), (), s32[]{:S(2)}) async-start(), calls=%async_computation.9 | async-start | bytes 12582912 | tf_op jit(solution)/shard_map/psum | solution.py:288
  744.0 25.1 %copy-start.55 = (u32[32]{0:T(128)S(1)}, u32[32]{0:T(128)}, u32[]{:S(2)}) copy-start(u32[32]{0:T(128)} %constant.93) | copy-start | bytes 388
  744.0 26.4 %copy-start.20 = (f32[48,16,4]{2,1,0:T(8,128)S(1)}, f32[48,16,4]{2,1,0:T(8,128)}, u32[]{:S(2)}) copy-start(f32[48,16,4]{2,1,0:T(8,128)} %copy-done.19) | copy-start | bytes 36868
  744.0 26.4 %copy-start.25 = (f32[48,16,4]{2,1,0:T(8,128)S(1)}, f32[48,16,4]{2,1,0:T(8,128)}, u32[]{:S(2)}) copy-start(f32[48,16,4]{2,1,0:T(8,128)} %get-tuple-element.209) | copy-start | bytes 36868
  744.0 26.4 %copy-start.46 = (f32[512]{0:T(512)S(1)}, f32[512]{0:T(512)}, u32[]{:S(2)}) copy-start(f32[512]{0:T(512)} %param.29) | copy-start | bytes 6148
  776.0 14.3 %slice-start.2 = ((s8[6291456]{0:T(1024)(128)(4,1)}), s8[2097152]{0:T(1024)(128)(4,1)S(1)}, s32[]{:S(2)}) async-start(s8[6291456]{0:T(1024)(128)(4,1)} %bitcast.168), calls=%async_computation.12 | async-start | bytes 4194304
  805.5 557.9 %all-reduce.16.cloned.1.call-start = ((), (), s32[]{:S(2)}) async-start(), calls=%async_computation.8 | async-start | bytes 4194304 | tf_op jit(solution)/shard_map/psum | solution.py:274
  1179.2 110.2 %copy-start.41 = (s32[1536]{0:T(1024)S(1)}, s32[1536]{0:T(1024)}, u32[]{:S(2)}) copy-start(s32[1536]{0:T(1024)} %copy-done.40) | copy-start | bytes 18436
  1331.0 41.0 %copy-start.24 = (f32[512,1024]{1,0:T(8,128)S(1)}, f32[512,1024]{1,0:T(8,128)}, u32[]{:S(2)}) copy-start(f32[512,1024]{1,0:T(8,128)} %get-tuple-element.383) | copy-start | bytes 6291460
  1363.4 11.2 copy-start.1
  (59 other events, 275.7 us)
Sparse Core Ops, SparseCore 0:
  46.2 47.6 all-gather.2
  101.9 45.2 all-gather.4
  242.1 162.9 all-reduce.11
  444.5 153.1 all-reduce.13
  805.6 207.0 all-reduce.17
  1183.9 179.4 all-reduce.15
where the time goes:
time: 1390 us; the launch traced here: 1380 us
  blocking collectives  516 us (37%)
  waiting for transfers between devices  394 us (28%)
  local copies, waits for them, and re-layouts  220 us (16%)
  matrix products  136 us (10%)
  other arithmetic  80.5 us (6%)
  starting transfers between devices  18.5 us (1%)
  between operations  16 us (1%)
    unnamed x1, blocking collectives  290 us
    psum x1, waiting for transfers between devices, layer_pass(): d_normed_two = lax.psum(d_normed_two, 'gy')  131 us
    psum x1, blocking collectives, per_device(): lax.psum((query_part, key_part, value_part, out_part_grad, second_gain_pa...  102 us
    all_to_all x1, blocking collectives, per_device(): lax.all_to_all(cot_all, 'gx', split_axis=0, concat_axis=1, tiled=True)  85.4 us
    psum x1, waiting for transfers between devices, layer_pass(): branch = lax.psum(branch, 'gy')  67 us
    all_to_all x1, waiting for transfers between devices, per_device(): lax.all_to_all(grad_seq, 'gx', split_axis=1, concat_axis=0, tiled=True)  58.3 us
    all_to_all x1, waiting for transfers between devices, per_device(): lax.all_to_all(token_all, 'gx', split_axis=0, concat_axis=1, tiled=True)  57.1 us
    all_gather x1, waiting for transfers between devices, per_device(): lax.all_gather(tokens, 'gy', axis=0, tiled=True)  47.8 us
  transfers between devices with their start and end apart: 9, of which 6 were waited for; matrix products, arithmetic and copies ran while one was open for 24% of the time, Pallas kernels for 0%

commit v1 on v0

--- a/solution.py
+++ b/solution.py
@@ -7,6 +7,18 @@
 EPSILON = 1e-05
 FLOAT = jnp.float32
 BFLOAT = jnp.bfloat16
+
+
+def sent_to_each(shard, axis, split, join):
+    ways, here = (lax.axis_size(axis), lax.axis_index(axis))
+    width = shard.shape[split] // ways
+    turned = jnp.roll(shard, -here * width, axis=split)
+    got = [lax.slice_in_dim(turned, 0, width, axis=split)]
+    for far in range(1, ways):
+        sent = lax.slice_in_dim(turned, far * width, (far + 1) * width, axis=split)
+        got.append(lax.ppermute(sent, axis, [(d, (d + far) % ways) for d in range(ways)]))
+    line = jnp.concatenate(got[::-1], axis=join)
+    return jnp.roll(line, (here + 1) * got[0].shape[join], axis=join)
 
 
 def norm_rows(values, gain, bias):
@@ -245,7 +257,7 @@
     out_seq, grad_seq, parts = layer_pass(seq_tokens, seq_cot, seg_rows, weights)
     out_moved, grad_moved = (
         lax.all_to_all(out_seq, "gx", split_axis=1, concat_axis=0, tiled=True),
-        lax.all_to_all(grad_seq, "gx", split_axis=1, concat_axis=0, tiled=True),
+        sent_to_each(grad_seq, "gx", 1, 0),
     )
     out_frames, grad_frames = (
         lax.psum_scatter(out_moved, "gy", scatter_dimension=0, tiled=True),

time: 1390 us -> 1440 us (1.036)
  blocking collectives: 516 us -> 466 us
  starting transfers between devices: 18.5 us -> 59 us
  waiting for transfers between devices: 394 us -> 423 us
    ppermute x0 -> x15, waiting for transfers between devices: none -> 145 us  [sent_to_each(): lax.ppermute(sent, axis, [(d, (d + far) % ways) for d in range(ways)])]
    all_to_all x1 -> x0, waiting for transfers between devices: 58.3 us -> none  [per_device(): lax.all_to_all(grad_seq, 'gx', split_axis=1, concat_axis=0, tiled=True)]
    psum x1, waiting for transfers between devices: 131 us -> 74.8 us  [layer_pass(): d_normed_two = lax.psum(d_normed_two, 'gy')]
    ppermute x0 -> x15, starting transfers between devices: none -> 46.9 us  [sent_to_each(): lax.ppermute(sent, axis, [(d, (d + far) % ways) for d in range(ways)])]
    psum x1, blocking collectives: 102 us -> 71.6 us  [per_device(): lax.psum((query_part, key_part, value_part, out_part_grad, second_gain_pa...]
    unnamed x1, blocking collectives: 290 us -> 271 us
  transfers between devices with their start and end apart: 9 -> 23, of which waited for: 6 -> 15; matrix products, arithmetic and copies ran while one was open for 24% -> 25% of each run, Pallas kernels for 0% -> 0%
where the time goes in v1:
time: 1440 us
  blocking collectives  466 us (32%)
  waiting for transfers between devices  423 us (29%)
  local copies, waits for them, and re-layouts  232 us (16%)
  matrix products  149 us (10%)
  other arithmetic  90.7 us (6%)
  starting transfers between devices  59 us (4%)
  between operations  15.9 us (1%)
    unnamed x1, blocking collectives  271 us
    ppermute x15, waiting for transfers between devices, sent_to_each(): lax.ppermute(sent, axis, [(d, (d + far) % ways) for d in range(ways)])  145 us
    all_to_all x1, blocking collectives, per_device(): lax.all_to_all(cot_all, 'gx', split_axis=0, concat_axis=1, tiled=True)  85.4 us
    psum x1, waiting for transfers between devices, layer_pass(): d_normed_two = lax.psum(d_normed_two, 'gy')  74.8 us
    psum x1, blocking collectives, per_device(): lax.psum((query_part, key_part, value_part, out_part_grad, second_gain_pa...  71.6 us
    psum x1, waiting for transfers between devices, layer_pass(): branch = lax.psum(branch, 'gy')  66.8 us
    all_to_all x1, waiting for transfers between devices, per_device(): lax.all_to_all(token_all, 'gx', split_axis=0, concat_axis=1, tiled=True)  56.5 us
    all_gather x1, waiting for transfers between devices, per_device(): lax.all_gather(tokens, 'gy', axis=0, tiled=True)  47.8 us
  transfers between devices with their start and end apart: 23, of which 15 were waited for; matrix products, arithmetic and copies ran while one was open for 25% of the time, Pallas kernels for 0%

profile of v1, /device:TPU:0, one launch (start us, length us, event | category | flops | bytes accessed | tf_op | source)
XLA Modules:
  0.0 1436.3 jit_solution(3040440072022588254)
XLA Ops:
  9.6 9.8 eq.91
  19.4 19.9 %eq.92 = s32[1536,1024]{1,0:T(8,128)} reshape(s32[384,4,32,32]{3,2,1,0:T(8,128)} %eq.91) | data formatting | bytes 12582912 | tf_op jit(solution)/shard_map/eq | solution.py:222
  46.7 47.8 %all-gather.3.cloned.1.call-done = bf16[768,4,512]{2,1,0:T(4,128)(2,1)} async-done(((bf16[384,4,512]{2,1,0:T(4,128)(2,1)}), bf16[768,4,512]{2,1,0:T(4,128)(2,1)}) %all-gather.3.cloned.1.call-update) | async-done | bytes 3145744 | tf_op jit(solution)/shard_map/all_gather | solution.py:233
  103.1 56.5 %all-to-all-done = bf16[768,4,512]{2,1,0:T(4,128)(2,1)} async-done(((bf16[768,4,512]{2,1,0:T(4,128)(2,1)}), bf16[768,4,512]{2,1,0:T(4,128)(2,1)}, u32[]{:S(2)}, u32[]{:S(2)}) %all-to-all-start) | async-done | bytes 3145760 | tf_op jit(solution)/shard_map/all_to_all | solution.py:237
  194.0 58.4 %while.24 = (s32[]{:T(128)}, bf16[6,8,64,256]{3,2,1,0:T(8,128)(2,1)}, bf16[6,8,64,256]{3,2,1,0:T(8,128)(2,1)}, s32[6,8,64]{2,1,0:T(8,128)}, bf16[6,8,64,256]{3,2...) while((s32[]{:T(128)}, bf16[6,8,64,256]{3,2,1,0:T(8,128)(2,1)}, ...), condition=%wide.region_5.6_spmd, body=%wide.region_2.5_spmd.sunk | while | flops 34674816 | bytes 9009281 | solution.py:127
  257.5 85.4 %all_to_all.42 = bf16[768,4,512]{2,1,0:T(4,128)(2,1)S(1)} all-to-all(bf16[768,4,512]{2,1,0:T(4,128)(2,1)} %all-gather.5.cloned.1.call-done), channel_id=1, replica_groups=mesh['gx'=16,'gy'=2] {'gx'}, dimensions={0} | all-to-all | bytes 6291456 | tf_op jit(solution)/shard_map/all_to_all | solution.py:238
  353.8 66.8 %all-reduce.12.cloned.1.call-done = f32[3072,512]{1,0:T(8,128)} async-done(((f32[3072,512]{1,0:T(8,128)}), f32[3072,512]{1,0:T(8,128)}) %all-reduce.12.cloned.1.call-update) | async-done | bytes 6291472 | tf_op jit(solution)/shard_map/psum | solution.py:132
  428.2 10.0 multiply_convert_fusion
  438.1 13.3 convert_reduce_fusion
  460.9 9.8 iota_compare_fusion.2
  470.7 15.2 %eq.103 = pred[1536,1024]{1,0:T(32,128)(4,1)} reshape(pred[384,4,32,32]{3,2,1,0:T(32,128)(4,1)} %iota_compare_fusion.2) | data formatting | bytes 3145728 | tf_op jit(solution)/shard_map/eq | solution.py:222
  498.4 10.0 multiply_add_fusion
  538.4 74.8 %all-reduce.14.cloned.1.call-done = f32[3072,512]{1,0:T(8,128)} async-done(((f32[3072,512]{1,0:T(8,128)}), f32[3072,512]{1,0:T(8,128)}) %all-reduce.14.cloned.1.call-update) | async-done | bytes 6291472 | tf_op jit(solution)/shard_map/psum | solution.py:149
  634.0 105.1 %while.25 = (s32[]{:T(128)}, bf16[6,8,64,256]{3,2,1,0:T(8,128)(2,1)}, bf16[6,8,64,256]{3,2,1,0:T(8,128)(2,1)}, bf16[6,8,64,256]{3,2,1,0:T(8,128)(2,1)}, bf16[6,8...) while((s32[]{:T(128)}, ...), condition=%wide.region_17.18_spmd, body=%wide.region_13.17_spmd.sunk | while | flops 86839424 | bytes 17954980 | solution.py:156
  787.5 39.0 %collective-permute-done.1 = f32[48,4,512]{2,1,0:T(4,128)S(1)} collective-permute-done((f32[48,4,512]{2,1,0:T(4,128)}, f32[48,4,512]{2,1,0:T(4,128)S(1)}, u32[]{:S(2)}, u32[]{:S(2)}) %collective-permute-start.1) | collective-permute-done | bytes 393248 | tf_op jit(solution)/shard_map/ppermute | solution.py:19
  832.0 11.3 collective-permute-done.4
  843.4 12.2 collective-permute-done.5
  865.4 32.0 %collective-permute-start.10 = (f32[48,4,512]{2,1,0:T(4,128)}, f32[48,4,512]{2,1,0:T(4,128)S(1)}, u32[]{:S(2)}, u32[]{:S(2)}) collective-permute-start(f32[48,4,512]{2,1,0:T(4,128)} %get-tuple-element.213), channel_id=1, source_target_pairs={{0,10},{2,12},{4,14},{6,16},{8,18},{10,20},{12,22},{14,24},{16,26}... | collective-permute-start | bytes 1179656 | tf_op jit(solution)/shard_map/ppermute | solution.py:19
  897.5 39.5 %collective-permute-done.7 = f32[48,4,512]{2,1,0:T(4,128)S(1)} collective-permute-done((f32[48,4,512]{2,1,0:T(4,128)}, f32[48,4,512]{2,1,0:T(4,128)S(1)}, u32[]{:S(2)}, u32[]{:S(2)}) %collective-permute-start.7) | collective-permute-done | bytes 393248 | tf_op jit(solution)/shard_map/ppermute | solution.py:19
  937.1 19.7 %collective-permute-done.8 = f32[48,4,512]{2,1,0:T(4,128)S(1)} collective-permute-done((f32[48,4,512]{2,1,0:T(4,128)}, f32[48,4,512]{2,1,0:T(4,128)S(1)}, u32[]{:S(2)}, u32[]{:S(2)}) %collective-permute-start.8) | collective-permute-done | bytes 393248 | tf_op jit(solution)/shard_map/ppermute | solution.py:19
  989.3 270.8 %all-reduce.19 = (bf16[768,4,512]{2,1,0:T(4,128)(2,1)}, bf16[768,4,512]{2,1,0:T(4,128)(2,1)}) all-reduce(f32[768,4,512]{2,1,0:T(4,128)} %bitcast.170, f32[768,4,512]{2,1,0:T(4,128)} %constant_dynamic-slice_fusion.7), channel_id=2, replica_groups=mesh['gx'=16,'gy'=2] {'gy'}, use_global_device_ids=true, to_apply=%region_9.10.clone | all-reduce | flops 3145728 | bytes 18874368
  1273.5 71.6 %all-reduce.3 = (f32[512]{0:T(512)}, f32[512]{0:T(512)}, f32[1024]{0:T(1024)}, f32[512]{0:T(512)}) all-reduce(f32[512]{0:T(512)S(1)} %get-tuple-element.146, f32[512]{0:T(512)S(1)} %get-tuple-element.150, f32[1024]{0:T(1024)S(1)} %copy-done.44, f32[512]{0:T(512)S(1)} %convert_reduce_fusion.1), channel_id=1, replica_groups=mesh['gx'=16,'gy'=2] {'gx'}, use_global_device_ids=true, to_apply=%region_32.33 | all-reduce | flops 2560 | bytes 20480 | tf_op jit(solution)/shard_map/psum | solution.py:300
  1345.7 38.0 %all-reduce.2 = (f32[18,512]{1,0:T(8,128)}, f32[512]{0:T(512)}, f32[512]{0:T(512)}) all-reduce(f32[18,512]{1,0:T(8,128)S(1)} %fusion.34, f32[512]{0:T(512)S(1)} %get-tuple-element.148, f32[512]{0:T(512)S(1)} %get-tuple-element.151), channel_id=1, replica_groups=mesh['gx'=16,'gy'=2] {'gx','gy'}, use_global_device_ids=true, to_apply=%region_22.23 | all-reduce | flops 10240 | bytes 81920 | tf_op jit(solution)/shard_map/psum | solution.py:286
  1386.7 31.3 %all-reduce.16.cloned.1.call-done = f32[1024,512]{1,0:T(8,128)} async-done(((f32[1024,512]{1,0:T(8,128)}), f32[1024,512]{1,0:T(8,128)}) %all-reduce.16.cloned.1.call-update) | async-done | bytes 2097168 | tf_op jit(solution)/shard_map/psum | solution.py:286
  (516 shorter events, 434.6 us)
Async XLA Ops:
  7.2 420.9 %copy-start = (bf16[512,1024]{1,0:T(8,128)(2,1)S(1)}, bf16[512,1024]{1,0:T(8,128)(2,1)}, u32[]{:S(2)}) copy-start(bf16[512,1024]{1,0:T(8,128)(2,1)} %param.36) | copy-start | bytes 3145732
  7.2 87.3 %all-gather.3.cloned.1.call-start = ((), (), s32[]{:S(2)}) async-start(), calls=%async_computation.3 | async-start | bytes 4718592 | tf_op jit(solution)/shard_map/all_gather | solution.py:233
  94.5 65.1 %all-to-all-start = ((bf16[768,4,512]{2,1,0:T(4,128)(2,1)}), bf16[768,4,512]{2,1,0:T(4,128)(2,1)}, u32[]{:S(2)}, u32[]{:S(2)}) async-start(bf16[768,4,512]{2,1,0:T(4,128)(2,1)} %all-gather.3.cloned.1.call-done), calls=%async_computation | async-start | bytes 6291456 | tf_op jit(solution)/shard_map/all_to_all | solution.py:237
  100.2 157.4 %all-gather.5.cloned.1.call-start = ((), (), s32[]{:S(2)}) async-start(), calls=%async_computation.5 | async-start | bytes 4718592 | tf_op jit(solution)/shard_map/all_gather | solution.py:234
  100.9 319.7 %all-reduce.12.cloned.1.call-start = ((), (), s32[]{:S(2)}) async-start(), calls=%async_computation.4 | async-start | bytes 12582912 | tf_op jit(solution)/shard_map/psum | solution.py:132
  257.4 355.7 %all-reduce.14.cloned.1.call-start = ((), (), s32[]{:S(2)}) async-start(), calls=%async_computation.6 | async-start | bytes 12582912 | tf_op jit(solution)/shard_map/psum | solution.py:149
  514.7 464.9 %all-to-all-start.1 = ((f32[48,64,512]{2,0,1:T(8,128)}), f32[48,64,512]{2,0,1:T(8,128)}, u32[]{:S(2)}, u32[]{:S(2)}) async-start(f32[48,64,512]{2,0,1:T(8,128)} %copy.106), calls=%async_computation.1 | async-start | bytes 12582912 | tf_op jit(solution)/shard_map/all_to_all | solution.py:259
  520.4 866.3 %all-reduce.18.cloned.1.call-start = ((), (), s32[]{:S(2)}) async-start(), calls=%async_computation.8 | async-start | bytes 12582912 | tf_op jit(solution)/shard_map/psum | solution.py:300
  772.1 13.9 collective-permute-start
  781.2 45.4 %collective-permute-start.3 = (f32[48,4,512]{2,1,0:T(4,128)}, f32[48,4,512]{2,1,0:T(4,128)S(1)}, u32[]{:S(2)}, u32[]{:S(2)}) collective-permute-start(f32[48,4,512]{2,1,0:T(4,128)} %get-tuple-element.220), channel_id=1, source_target_pairs={{0,24},{2,26},{4,28},{6,30},{8,0},{10,2},{12,4},{14,6},{16,8},{18,... | collective-permute-start | bytes 1179656 | tf_op jit(solution)/shard_map/ppermute | solution.py:19
  782.3 44.2 %collective-permute-start.2 = (f32[48,4,512]{2,1,0:T(4,128)}, f32[48,4,512]{2,1,0:T(4,128)S(1)}, u32[]{:S(2)}, u32[]{:S(2)}) collective-permute-start(f32[48,4,512]{2,1,0:T(4,128)} %get-tuple-element.221), channel_id=1, source_target_pairs={{0,26},{2,28},{4,30},{6,0},{8,2},{10,4},{12,6},{14,8},{16,10},{18,... | collective-permute-start | bytes 1179656 | tf_op jit(solution)/shard_map/ppermute | solution.py:19
  782.3 44.2 %collective-permute-start.1 = (f32[48,4,512]{2,1,0:T(4,128)}, f32[48,4,512]{2,1,0:T(4,128)S(1)}, u32[]{:S(2)}, u32[]{:S(2)}) collective-permute-start(f32[48,4,512]{2,1,0:T(4,128)} %get-tuple-element.222), channel_id=1, source_target_pairs={{0,28},{2,30},{4,0},{6,2},{8,4},{10,6},{12,8},{14,10},{16,12},{18,... | collective-permute-start | bytes 1179656 | tf_op jit(solution)/shard_map/ppermute | solution.py:19
  785.6 186.9 %collective-permute-start.14 = (f32[48,4,512]{2,1,0:T(4,128)S(1)}, f32[48,4,512]{2,1,0:T(4,128)S(1)}, u32[]{:S(2)}, u32[]{:S(2)}) collective-permute-start(f32[48,4,512]{2,1,0:T(4,128)S(1)} %get-tuple-element.209), channel_id=1, source_target_pairs={{0,2},{2,4},{4,6},{6,8},{8,10},{10,12},{12,14},{14,16},{16,18},{18... | collective-permute-start | bytes 1179656 | tf_op jit(solution)/shard_map/ppermute | solution.py:19
  785.9 632.1 %all-reduce.16.cloned.1.call-start = ((), (), s32[]{:S(2)}) async-start(), calls=%async_computation.7 | async-start | bytes 4194304 | tf_op jit(solution)/shard_map/psum | solution.py:286
  786.0 57.3 %collective-permute-start.4 = (f32[48,4,512]{2,1,0:T(4,128)}, f32[48,4,512]{2,1,0:T(4,128)S(1)}, u32[]{:S(2)}, u32[]{:S(2)}) collective-permute-start(f32[48,4,512]{2,1,0:T(4,128)} %get-tuple-element.219), channel_id=1, source_target_pairs={{0,22},{2,24},{4,26},{6,28},{8,30},{10,0},{12,2},{14,4},{16,6},{18... | collective-permute-start | bytes 1179656 | tf_op jit(solution)/shard_map/ppermute | solution.py:19
  826.5 29.1 %collective-permute-start.5 = (f32[48,4,512]{2,1,0:T(4,128)}, f32[48,4,512]{2,1,0:T(4,128)S(1)}, u32[]{:S(2)}, u32[]{:S(2)}) collective-permute-start(f32[48,4,512]{2,1,0:T(4,128)} %get-tuple-element.218), channel_id=1, source_target_pairs={{0,20},{2,22},{4,24},{6,26},{8,28},{10,30},{12,0},{14,2},{16,4},{1... | collective-permute-start | bytes 1179656 | tf_op jit(solution)/shard_map/ppermute | solution.py:19
  826.5 38.9 %collective-permute-start.6 = (f32[48,4,512]{2,1,0:T(4,128)}, f32[48,4,512]{2,1,0:T(4,128)S(1)}, u32[]{:S(2)}, u32[]{:S(2)}) collective-permute-start(f32[48,4,512]{2,1,0:T(4,128)} %get-tuple-element.217), channel_id=1, source_target_pairs={{0,18},{2,20},{4,22},{6,24},{8,26},{10,28},{12,30},{14,0},{16,2},{... | collective-permute-start | bytes 1179656 | tf_op jit(solution)/shard_map/ppermute | solution.py:19
  826.7 110.4 %collective-permute-start.7 = (f32[48,4,512]{2,1,0:T(4,128)}, f32[48,4,512]{2,1,0:T(4,128)S(1)}, u32[]{:S(2)}, u32[]{:S(2)}) collective-permute-start(f32[48,4,512]{2,1,0:T(4,128)} %get-tuple-element.216), channel_id=1, source_target_pairs={{0,16},{2,18},{4,20},{6,22},{8,24},{10,26},{12,28},{14,30},{16,0},... | collective-permute-start | bytes 1179656 | tf_op jit(solution)/shard_map/ppermute | solution.py:19
  843.3 113.5 %collective-permute-start.8 = (f32[48,4,512]{2,1,0:T(4,128)}, f32[48,4,512]{2,1,0:T(4,128)S(1)}, u32[]{:S(2)}, u32[]{:S(2)}) collective-permute-start(f32[48,4,512]{2,1,0:T(4,128)} %get-tuple-element.215), channel_id=1, source_target_pairs={{0,14},{2,16},{4,18},{6,20},{8,22},{10,24},{12,26},{14,28},{16,30}... | collective-permute-start | bytes 1179656 | tf_op jit(solution)/shard_map/ppermute | solution.py:19
  855.5 105.1 %collective-permute-start.9 = (f32[48,4,512]{2,1,0:T(4,128)}, f32[48,4,512]{2,1,0:T(4,128)S(1)}, u32[]{:S(2)}, u32[]{:S(2)}) collective-permute-start(f32[48,4,512]{2,1,0:T(4,128)} %get-tuple-element.214), channel_id=1, source_target_pairs={{0,12},{2,14},{4,16},{6,18},{8,20},{10,22},{12,24},{14,26},{16,28}... | collective-permute-start | bytes 1179656 | tf_op jit(solution)/shard_map/ppermute | solution.py:19
  865.4 96.8 %collective-permute-start.10 = (f32[48,4,512]{2,1,0:T(4,128)}, f32[48,4,512]{2,1,0:T(4,128)S(1)}, u32[]{:S(2)}, u32[]{:S(2)}) collective-permute-start(f32[48,4,512]{2,1,0:T(4,128)} %get-tuple-element.213), channel_id=1, source_target_pairs={{0,10},{2,12},{4,14},{6,16},{8,18},{10,20},{12,22},{14,24},{16,26}... | collective-permute-start | bytes 1179656 | tf_op jit(solution)/shard_map/ppermute | solution.py:19
  937.0 25.2 %collective-permute-start.11 = (f32[48,4,512]{2,1,0:T(4,128)}, f32[48,4,512]{2,1,0:T(4,128)S(1)}, u32[]{:S(2)}, u32[]{:S(2)}) collective-permute-start(f32[48,4,512]{2,1,0:T(4,128)} %get-tuple-element.212), channel_id=1, source_target_pairs={{0,8},{2,10},{4,12},{6,14},{8,16},{10,18},{12,20},{14,22},{16,24},... | collective-permute-start | bytes 1179656 | tf_op jit(solution)/shard_map/ppermute | solution.py:19
  956.8 9.2 collective-permute-start.12
  960.7 11.8 collective-permute-start.13
  (65 other events, 641.2 us)
Sparse Core Ops, SparseCore 0:
  46.8 47.6 all-gather.2
  102.5 45.2 all-gather.4
  257.6 162.9 all-reduce.11
  460.0 153.1 all-reduce.13
  786.1 245.6 all-reduce.17
  1270.3 147.6 all-reduce.15
